TPU v7x, 512 devices: a whole 4x4x16 slice. The times are simulated.
512 devices in a mesh: gx: 16 (over z), gy: 32 (over x, y, core).
Axes of the slice: x: 4, y: 4, z: 16, core: 2. Of those that a mesh axis runs over, the one named last changes fastest.
Arguments:
- particles: bfloat16 [32768, 4096], P(('gx', 'gy')), may hold values from -6 to 6
- references: bfloat16 [16, 12, 4096], P('gx'), may hold values from -1 to 1
- slot_class: int32 [16], replicated, may hold values from 0 to 15, each once
- log_prior: float32 [16], replicated, may hold values from -2 to 2
- shift_offsets: int32 [8, 2], replicated, may hold values from -8 to 8
- group_ids: int32 [32768], P(('gx', 'gy')), may hold values from 0 to 127
- ctf_table: float32 [128, 2048], replicated, may hold values from -1 to 1
- noise_power: float32 [2048], replicated, may hold values from 0.5 to 2
Outputs:
- class_sums: float32 [16, 12, 4096], P('gx')
- ctf_power: float32 [16, 2048], P('gx')
- log_evidence: float32 [], replicated
Inputs may be any that keep to these rules, and one draw needn't show every extreme that they name: `slot_class`: each class id stands at exactly one slot.
All inputs are finite; a program needn't handle non-finite values.
Results may differ from a plain program's by a relative error of at most 0.006.
Values may be sent and summed in bfloat16 or wider, within the bound.
A program may use at most 64 MiB of HBM per device.

v0:
```python
import functools
import jax
import jax.numpy as jnp
from jax import lax
from jax.sharding import Mesh
from jax.sharding import PartitionSpec as P

L = 64
R = 12
NS = 8
G = 128
HALF = 2048
FR = 4096
GY = ("gy_0", "gy_1", "gy_2")
GX_GY = ("gx", "gy_0", "gy_1", "gy_2")


def in_blocks(shard, dim, length):
    before, after = (shard.shape[:dim], shard.shape[dim + 1 :])
    return jnp.moveaxis(shard.reshape(*before, length, -1, *after), dim, 0)


def summed_on_arrival(shard, axis, dim):
    tiles = in_blocks(shard, dim, lax.axis_size(axis))
    arrived = lax.all_to_all(tiles, axis, split_axis=0, concat_axis=0, tiled=True)
    return arrived.sum(axis=0)


def gathered_total(shard, axis):
    return lax.all_gather(shard, axis).sum(0)


def over_axes(shard, axes):
    return functools.reduce(lax.psum, axes, shard)


def phase_tables(shift_offsets, edge_len):
    half_size = edge_len * edge_len // 2
    freq_index = jnp.arange(half_size, dtype=jnp.int32)
    row_freq = freq_index // (edge_len // 2)
    col_freq = freq_index % (edge_len // 2)
    phase_turns = jnp.mod(
        row_freq[None, :] * shift_offsets[:, 0:1] + col_freq[None, :] * shift_offsets[:, 1:2],
        edge_len,
    )
    angles = phase_turns.astype(jnp.float32) * (2.0 * jnp.pi / edge_len)
    return (jnp.cos(angles), jnp.sin(angles))


def spectra(particles, edge_len):
    rows_here = particles.shape[0]
    half_side = edge_len // 2
    images = particles.astype(jnp.float32).reshape(rows_here * edge_len, edge_len)
    pixel_index = jnp.arange(edge_len, dtype=jnp.int32)
    column_turns = jnp.mod(pixel_index[:, None] * pixel_index[None, :half_side], edge_len).astype(
        jnp.float32
    ) * (2.0 * jnp.pi / edge_len)
    column_table = jnp.concatenate([jnp.cos(column_turns), -jnp.sin(column_turns)], axis=1)
    partial_x = jnp.dot(
        images, column_table, precision=lax.Precision.HIGHEST, preferred_element_type=jnp.float32
    )
    partial_x = partial_x.reshape(rows_here, edge_len, edge_len)
    row_turns = jnp.mod(pixel_index[:, None] * pixel_index[None, :], edge_len).astype(
        jnp.float32
    ) * (2.0 * jnp.pi / edge_len)
    with_cos = jnp.einsum(
        "uy,pyw->puw", jnp.cos(row_turns), partial_x, precision=lax.Precision.HIGHEST
    )
    with_sin = jnp.einsum(
        "uy,pyw->puw", jnp.sin(row_turns), partial_x, precision=lax.Precision.HIGHEST
    )
    real_part = (with_cos[..., :half_side] + with_sin[..., half_side:]) / edge_len
    imag_part = (with_cos[..., half_side:] - with_sin[..., :half_side]) / edge_len
    return (real_part.reshape(rows_here, -1), imag_part.reshape(rows_here, -1))


def shards(
    particles, references, slot_class, log_prior, shift_offsets, group_ids, ctf_table, noise_power
):
    rows_here = particles.shape[0]
    classes = lax.axis_size("gx") * references.shape[0]
    row_width = R * NS
    real_part, imag_part = spectra(particles, L)
    inv_noise = 1.0 / noise_power
    group_hot = (group_ids[:, None] == jnp.arange(G, dtype=jnp.int32)[None, :]).astype(jnp.float32)
    ctf_rows = jnp.dot(
        group_hot, ctf_table, precision=lax.Precision.HIGHEST, preferred_element_type=jnp.float32
    )
    whiten = ctf_rows * inv_noise
    weighted = jnp.concatenate([real_part * whiten, imag_part * whiten], axis=1).astype(
        jnp.bfloat16
    )
    data_power = jnp.sum((real_part * real_part + imag_part * imag_part) * inv_noise, axis=1)
    cosines, sine_table = phase_tables(shift_offsets, L)
    power_table = ctf_table * ctf_table * inv_noise
    blank = jnp.zeros((rows_here, classes * row_width), jnp.float32)
    piece = lax.all_gather(references, "gx", axis=0, tiled=True)

    def add_class(offset, table):
        stack_row = lax.dynamic_index_in_dim(piece, offset, 0, keepdims=False).astype(jnp.float32)
        stack_real = stack_row[:, :HALF]
        stack_imag = stack_row[:, HALF:]
        shifted_real = (
            stack_real[:, None, :] * cosines[None] + stack_imag[:, None, :] * sine_table[None]
        )
        shifted_imag = (
            stack_imag[:, None, :] * cosines[None] - stack_real[:, None, :] * sine_table[None]
        )
        shifted = (
            jnp.concatenate([shifted_real, shifted_imag], axis=2)
            .astype(jnp.bfloat16)
            .reshape(row_width, FR)
        )
        intersection = lax.dot_general(
            weighted, shifted, (((1,), (1,)), ((), ())), preferred_element_type=jnp.float32
        )
        amplitude = stack_real * stack_real + stack_imag * stack_imag
        ref_power = jnp.dot(
            power_table,
            amplitude.T,
            precision=lax.Precision.HIGHEST,
            preferred_element_type=jnp.float32,
        )
        own_power = jnp.dot(
            group_hot,
            ref_power,
            precision=lax.Precision.HIGHEST,
            preferred_element_type=jnp.float32,
        )
        logits = intersection.reshape(rows_here, R, NS) - 0.5 * own_power[:, :, None]
        return lax.dynamic_update_slice_in_dim(
            table, logits.reshape(rows_here, row_width), offset * row_width, 1
        )

    scores = lax.fori_loop(0, piece.shape[0], add_class, blank)
    slot_prior = jnp.sum(
        jnp.where(
            slot_class[:, None] == jnp.arange(classes, dtype=jnp.int32)[None, :],
            log_prior[None, :],
            0.0,
        ),
        axis=1,
    )
    logits = (
        scores.reshape(rows_here, classes, row_width)
        - 0.5 * data_power[:, None, None]
        + slot_prior[None, :, None]
    )
    row_max = jnp.max(logits, axis=(1, 2), keepdims=True)
    raised = jnp.exp(logits - row_max)
    normaliser = jnp.sum(raised, axis=(1, 2), keepdims=True)
    weights = raised / normaliser
    evidence = row_max[:, 0, 0] + jnp.log(normaliser[:, 0, 0])
    weights_low = weights.astype(jnp.bfloat16)
    group_weights = jnp.dot(
        jnp.sum(weights, axis=2).T,
        group_hot,
        precision=lax.Precision.HIGHEST,
        preferred_element_type=jnp.float32,
    )

    def class_terms(slot_index):
        weight_cols = lax.dynamic_index_in_dim(weights_low, slot_index, 1, keepdims=False)
        moment = lax.dot_general(
            weight_cols, weighted, (((0,), (0,)), ((), ())), preferred_element_type=jnp.float32
        )
        moment = moment.reshape(R, NS, FR)
        moment_real = moment[..., :HALF]
        moment_imag = moment[..., HALF:]
        back_real = jnp.sum(moment_real * cosines[None] - moment_imag * sine_table[None], axis=1)
        back_imag = jnp.sum(moment_imag * cosines[None] + moment_real * sine_table[None], axis=1)
        return jnp.concatenate([back_real, back_imag], axis=1)

    owned = summed_on_arrival(
        lax.map(
            lambda offset: class_terms(offset),
            jnp.arange(references.shape[0] * lax.axis_size("gx"), dtype=jnp.int32),
        ),
        "gx",
        0,
    )
    class_sums = gathered_total(owned, GY)
    totals, evidence_sum = (over_axes(group_weights, GX_GY), over_axes(jnp.sum(evidence), GX_GY))
    own_groups = lax.dynamic_slice_in_dim(totals, lax.axis_index("gx"), 1, 0)
    ctf_power = jnp.dot(
        own_groups,
        ctf_table * ctf_table,
        precision=lax.Precision.HIGHEST,
        preferred_element_type=jnp.float32,
    )
    log_evidence = evidence_sum / (rows_here * lax.axis_size("gx") * lax.axis_size(GY) * HALF)
    return (class_sums, ctf_power, log_evidence)


def solution(mesh):
    finer = Mesh(mesh.devices.reshape(mesh.shape["gx"], 4, 4, 2), ("gx", "gy_0", "gy_1", "gy_2"))
    in_specs = (P(GX_GY, None), P("gx", None, None), P(), P(), P(), P(GX_GY), P(), P())
    out_specs = (P("gx", None, None), P("gx", None), P())
    return jax.shard_map(
        shards, mesh=finer, in_specs=in_specs, out_specs=out_specs, check_vma=False
    )
```

profile of v0, /device:TPU:1, one launch (start us, length us, event | category | flops | bytes accessed | tf_op | source)
XLA Modules:
  0.0 449.0 jit_solution(14983572868372554271)
XLA Ops:
  8.1 2.1 reshape.117
  10.2 1.3 convolution_bitcast_fusion.1
  12.5 3.4 fusion.46
  15.9 3.4 fusion.49
  19.9 1.1 copy.47
  21.4 2.0 copy.49
  23.4 1.5 copy.50
  26.2 53.3 %all-gather.5.cloned.1.call-done = bf16[16,12,4096]{2,1,0:T(8,128)(2,1)} async-done(((bf16[1,12,4096]{2,1,0:T(8,128)(2,1)}), bf16[16,12,4096]{2,1,0:T(8,128)(2,1)}) %all-gather.5.cloned.1.call-update) | async-done | bytes 1572880 | tf_op jit(solution)/shard_map/all_gather | solution.py:97
  79.5 60.2 %while.27 = (s32[]{:T(128)}, f32[64,1536]{1,0:T(8,128)S(1)}, bf16[16,12,4096]{2,1,0:T(8,128)(2,1)}, bf16[64,4096]{1,0:T(8,128)(2,1)S(1)}, f32[128,2048]{1,0:T(8,...) while((s32[]{:T(128)}, f32[64,1536]{1,0:T(8,128)S(1)}, ...), condition=%wide.region_1.2_spmd.clone.clone, body=%wide.region_0.1_spmd.clone.clone.sunk | while | flops 92814080 | bytes 4696571 | solution.py:135
  79.6 0.9 bitcast_convert_fusion.2
  83.2 0.9 bitcast_convert_fusion.2
  87.0 0.9 bitcast_convert_fusion.2
  90.8 0.9 bitcast_convert_fusion.2
  94.6 0.9 bitcast_convert_fusion.2
  98.3 0.9 bitcast_convert_fusion.2
  102.1 0.9 bitcast_convert_fusion.2
  105.9 0.9 bitcast_convert_fusion.2
  109.7 0.9 bitcast_convert_fusion.2
  113.4 0.9 bitcast_convert_fusion.2
  117.2 0.9 bitcast_convert_fusion.2
  121.0 0.9 bitcast_convert_fusion.2
  140.8 72.5 %while.28 = (s32[]{:T(128)}, f32[16,12,4096]{2,1,0:T(8,128)}, s32[16]{0:T(128)S(1)}, bf16[64,16,96]{0,2,1:T(8,128)(2,1)S(1)}, bf16[64,4096]{1,0:T(8,128)(2,1)S(1...) while((s32[]{:T(128)}, f32[16,12,4096]{2,1,0:T(8,128)}, ...), condition=%wide.region_9.10_spmd.clone.clone, body=%wide.region_6.9_spmd.clone.clone.sunk | while | flops 52166660 | bytes 4629223 | solution.py:175
  213.3 5.5 %copy.54 = f32[16,1,12,4096]{3,1,2,0:T(1,128)S(1)} copy(f32[16,1,12,4096]{3,2,0,1:T(8,128)} %bitcast.10) | data formatting | bytes 6291456 | tf_op jit(solution)/shard_map/reshape | solution.py:20
  218.7 134.6 %all_to_all.5 = f32[16,1,12,4096]{3,1,2,0:T(1,128)S(1)} all-to-all(f32[16,1,12,4096]{3,1,2,0:T(1,128)S(1)} %copy.54), channel_id=1, replica_groups=mesh['gx'=16,'gy_0'=4,'gy_1'=4,'gy_2'=2] {'gx'}, dimensions={0} | all-to-all | bytes 6291456 | tf_op jit(solution)/shard_map/all_to_all | solution.py:25
  353.3 4.3 reduce_sum.86
  358.4 27.7 %all-reduce = (f32[16,128]{1,0:T(8,128)S(1)}, f32[]{:T(128)}) all-reduce(f32[16,128]{1,0:T(8,128)S(1)} %fusion.68, f32[]{:T(128)} %add_reduce_fusion.1), channel_id=1, replica_groups=mesh['gx'=16,'gy_0'=4,'gy_1'=4,'gy_2'=2] {'gx'}, use_global_device_ids=true, to_apply=%region_13.14 | all-reduce | flops 2049 | bytes 16392 | tf_op jit(solution)/shard_map/psum | solution.py:34
  386.1 9.8 %all-reduce.2 = (f32[16,128]{1,0:T(8,128)S(1)}, f32[]{:T(128)}) all-reduce(f32[16,128]{1,0:T(8,128)S(1)} %get-tuple-element.360, f32[]{:T(128)} %get-tuple-element.361), channel_id=1, replica_groups=mesh['gx'=16,'gy_0'=4,'gy_1'=4,'gy_2'=2] {'gy_0'}, use_global_device_ids=true, to_apply=%region_14.15 | all-reduce | flops 2049 | bytes 16392 | tf_op jit(solution)/shard_map/psum | solution.py:34
  395.8 9.3 %all-reduce.1 = (f32[16,128]{1,0:T(8,128)S(1)}, f32[]{:T(128)}) all-reduce(f32[16,128]{1,0:T(8,128)S(1)} %get-tuple-element.364, f32[]{:T(128)} %get-tuple-element.365), channel_id=1, replica_groups=mesh['gx'=16,'gy_0'=4,'gy_1'=4,'gy_2'=2] {'gy_1'}, use_global_device_ids=true, to_apply=%region_15.16 | all-reduce | flops 2049 | bytes 16392 | tf_op jit(solution)/shard_map/psum | solution.py:34
  405.1 25.2 %all-reduce.3 = (f32[16,128]{1,0:T(8,128)S(1)}, f32[]{:T(128)}) all-reduce(f32[16,128]{1,0:T(8,128)S(1)} %get-tuple-element.362, f32[]{:T(128)} %get-tuple-element.363), channel_id=1, replica_groups=mesh['gx'=16,'gy_0'=4,'gy_1'=4,'gy_2'=2] {'gy_2'}, use_global_device_ids=true, to_apply=%region_16.17 | all-reduce | flops 2049 | bytes 16392 | tf_op jit(solution)/shard_map/psum | solution.py:34
  431.0 2.5 fusion.54
  433.4 2.8 all-gather.7.cloned.1.call-done
  436.2 3.9 reduce.5
  (271 shorter events, 95.9 us)
Async XLA Ops:
  7.2 4.3 copy-start.1
  7.2 72.3 %all-gather.5.cloned.1.call-start = ((), (), s32[]{:S(2)}) async-start(), calls=%async_computation.1 | async-start | bytes 2228224 | tf_op jit(solution)/shard_map/all_gather | solution.py:97
  7.9 428.3 %all-gather.7.cloned.1.call-start = ((), (), s32[]{:S(2)}) async-start(), calls=%async_computation.2 | async-start | bytes 8650752 | tf_op jit(solution)/shard_map/all_gather | solution.py:30
  21.3 3.6 copy-start.4
  21.3 3.6 copy-start.5
  21.3 4.0 copy-start.2
  21.3 4.0 copy-start
  21.4 4.0 copy-start.3
Sparse Core Ops, SparseCore 0:
  10.1 69.3 all-gather.4
  357.7 78.4 all-gather.6
where the time goes:
time: 450 us; the launch traced here: 449 us
  blocking collectives  206 us (46%)
  other arithmetic  60.1 us (13%)
  waiting for transfers between devices  56.8 us (13%)
  matrix products  42.2 us (9%)
  local copies, waits for them, and re-layouts  34.8 us (8%)
  loops' own time  32.5 us (7%)
  between operations  16.1 us (4%)
    all_to_all x1, blocking collectives, summed_on_arrival(): lax.all_to_all(tiles, axis, split_axis=0, concat_axis=0, tiled=True)  135 us
    psum x4, blocking collectives, over_axes(): return functools.reduce(lax.psum, axes, shard)  71.9 us
    all_gather x1, waiting for transfers between devices, shards(): piece = lax.all_gather(references, 'gx', axis=0, tiled=True)  53.3 us
    another operation x1, loops' own time, shards(): lax.map(lambda offset: class_terms(offset), jnp.arange(references.shape[0...  31.4 us
    convert_element_type x16, other arithmetic, add_class(): lax.dynamic_index_in_dim(piece, offset, 0, keepdims=False)  14.8 us
    dot_general x16, matrix products, add_class(): jnp.dot(power_table, amplitude.T, precision=lax.Precision.HIGHEST, prefer...  14.7 us
    dynamic_update_slice x16, other arithmetic, shards(): lax.map(lambda offset: class_terms(offset), jnp.arange(references.shape[0...  11.7 us
    cos x32, other arithmetic, phase_tables(): return (jnp.cos(angles), jnp.sin(angles))  11 us
  transfers between devices with their start and end apart: 2, of which 2 were waited for; matrix products, arithmetic and copies ran while one was open for 5% of the time, Pallas kernels for 0%

commit v1 on v0

--- a/solution.py
+++ b/solution.py
@@ -94,7 +94,9 @@
     cosines, sine_table = phase_tables(shift_offsets, L)
     power_table = ctf_table * ctf_table * inv_noise
     blank = jnp.zeros((rows_here, classes * row_width), jnp.float32)
-    piece = lax.all_gather(references, "gx", axis=0, tiled=True)
+    piece = jnp.concatenate(
+        lax.all_to_all(jnp.stack([references] * lax.axis_size("gx")), "gx", 0, 0), axis=0
+    )
 
     def add_class(offset, table):
         stack_row = lax.dynamic_index_in_dim(piece, offset, 0, keepdims=False).astype(jnp.float32)

time: 450 us -> 492 us (1.093)
  waiting for transfers between devices: 56.8 us -> 75.4 us
  starting transfers between devices: 0.08 us -> 16 us
  blocking collectives: 206 us -> 212 us
    all_to_all x0 -> x1, waiting for transfers between devices: none -> 74.4 us  [shards(): lax.all_to_all(jnp.stack([references] * lax.axis_size('gx')), 'gx', 0, 0)]
    all_gather x1 -> x0, waiting for transfers between devices: 53.3 us -> none  [shards(): piece = lax.all_gather(references, 'gx', axis=0, tiled=True)]
    all_to_all x0 -> x1, starting transfers between devices: none -> 15.9 us  [shards(): lax.all_to_all(jnp.stack([references] * lax.axis_size('gx')), 'gx', 0, 0)]
    all_to_all x1, blocking collectives: 135 us -> 146 us  [summed_on_arrival(): lax.all_to_all(tiles, axis, split_axis=0, concat_axis=0, tiled=True)]
    psum x4, blocking collectives: 71.9 us -> 66.2 us  [over_axes(): return functools.reduce(lax.psum, axes, shard)]
  transfers between devices with their start and end apart: 2 -> 2, of which waited for: 2 -> 2; matrix products, arithmetic and copies ran while one was open for 5% -> 4% of each run, Pallas kernels for 0% -> 0%
where the time goes in v1:
time: 492 us; the launch traced here: 491 us
  blocking collectives  212 us (43%)
  waiting for transfers between devices  75.4 us (15%)
  other arithmetic  60.1 us (12%)
  matrix products  42.1 us (9%)
  local copies, waits for them, and re-layouts  36.6 us (7%)
  loops' own time  32.5 us (7%)
  between operations  16.1 us (3%)
  starting transfers between devices  16 us (3%)
    all_to_all x1, blocking collectives, summed_on_arrival(): lax.all_to_all(tiles, axis, split_axis=0, concat_axis=0, tiled=True)  146 us
    all_to_all x1, waiting for transfers between devices, shards(): lax.all_to_all(jnp.stack([references] * lax.axis_size('gx')), 'gx', 0, 0)  74.4 us
    psum x4, blocking collectives, over_axes(): return functools.reduce(lax.psum, axes, shard)  66.2 us
    another operation x1, loops' own time, shards(): lax.map(lambda offset: class_terms(offset), jnp.arange(references.shape[0...  31.4 us
    all_to_all x1, starting transfers between devices, shards(): lax.all_to_all(jnp.stack([references] * lax.axis_size('gx')), 'gx', 0, 0)  15.9 us
    convert_element_type x16, other arithmetic, add_class(): lax.dynamic_index_in_dim(piece, offset, 0, keepdims=False)  14.8 us
    dot_general x16, matrix products, add_class(): jnp.dot(power_table, amplitude.T, precision=lax.Precision.HIGHEST, prefer...  14.7 us
    dynamic_update_slice x16, other arithmetic, shards(): lax.map(lambda offset: class_terms(offset), jnp.arange(references.shape[0...  11.7 us
  transfers between devices with their start and end apart: 2, of which 2 were waited for; matrix products, arithmetic and copies ran while one was open for 4% of the time, Pallas kernels for 0%

profile of v1, /device:TPU:1, one launch (start us, length us, event | category | flops | bytes accessed | tf_op | source)
XLA Modules:
  0.0 491.1 jit_solution(672126156915585973)
XLA Ops:
  7.2 2.5 stack.2
  9.7 15.9 %all-to-all-start = ((bf16[16,1,12,4096]{3,2,1,0:T(8,128)(2,1)}), bf16[16,1,12,4096]{3,2,1,0:T(8,128)(2,1)}, u32[]{:S(2)}, u32[]{:S(2)}) async-start(bf16[16,1,12,4096]{3,2,1,0:T(8,128)(2,1)} %stack.2), calls=%async_computation | async-start | bytes 4194304 | tf_op jit(solution)/shard_map/all_to_all | solution.py:98
  25.7 1.1 reshape.124
  26.9 1.3 convolution_bitcast_fusion.1
  29.3 3.4 fusion.46
  32.7 3.4 fusion.49
  36.7 1.1 copy.47
  38.1 2.2 copy.49
  40.4 1.5 copy.50
  43.1 74.4 %all-to-all-done = bf16[16,1,12,4096]{3,2,1,0:T(8,128)(2,1)} async-done(((bf16[16,1,12,4096]{3,2,1,0:T(8,128)(2,1)}), bf16[16,1,12,4096]{3,2,1,0:T(8,128)(2,1)}, u32[]{:S(2)}, u32[]{:S(2)}) %all-to-all-start) | async-done | bytes 1572896 | tf_op jit(solution)/shard_map/all_to_all | solution.py:98
  117.5 60.2 %while.27 = (s32[]{:T(128)}, f32[64,1536]{1,0:T(8,128)S(1)}, bf16[16,12,4096]{2,1,0:T(8,128)(2,1)}, bf16[64,4096]{1,0:T(8,128)(2,1)S(1)}, f32[128,2048]{1,0:T(8,...) while((s32[]{:T(128)}, f32[64,1536]{1,0:T(8,128)S(1)}, ...), condition=%wide.region_1.2_spmd.clone.clone, body=%wide.region_0.1_spmd.clone.clone.sunk | while | flops 92814080 | bytes 4696571 | solution.py:137
  117.5 0.9 bitcast_convert_fusion.2
  121.2 0.9 bitcast_convert_fusion.2
  125.0 0.9 bitcast_convert_fusion.2
  128.8 0.9 bitcast_convert_fusion.2
  132.6 0.9 bitcast_convert_fusion.2
  136.3 0.9 bitcast_convert_fusion.2
  140.1 0.9 bitcast_convert_fusion.2
  143.9 0.9 bitcast_convert_fusion.2
  147.7 0.9 bitcast_convert_fusion.2
  151.3 0.9 bitcast_convert_fusion.2
  178.8 72.5 %while.28 = (s32[]{:T(128)}, f32[16,12,4096]{2,1,0:T(8,128)}, s32[16]{0:T(128)S(1)}, bf16[64,16,96]{0,2,1:T(8,128)(2,1)S(1)}, bf16[64,4096]{1,0:T(8,128)(2,1)S(1...) while((s32[]{:T(128)}, f32[16,12,4096]{2,1,0:T(8,128)}, ...), condition=%wide.region_9.10_spmd.clone.clone, body=%wide.region_6.9_spmd.clone.clone.sunk | while | flops 52166660 | bytes 4629223 | solution.py:177
  251.3 5.5 %copy.54 = f32[16,1,12,4096]{3,1,2,0:T(1,128)S(1)} copy(f32[16,1,12,4096]{3,2,0,1:T(8,128)} %bitcast.12) | data formatting | bytes 6291456 | tf_op jit(solution)/shard_map/reshape | solution.py:20
  256.7 146.1 %all_to_all.10 = f32[16,1,12,4096]{3,1,2,0:T(1,128)S(1)} all-to-all(f32[16,1,12,4096]{3,1,2,0:T(1,128)S(1)} %copy.54), channel_id=1, replica_groups=mesh['gx'=16,'gy_0'=4,'gy_1'=4,'gy_2'=2] {'gx'}, dimensions={0} | all-to-all | bytes 6291456 | tf_op jit(solution)/shard_map/all_to_all | solution.py:25
  402.9 4.3 reduce_sum.86
  408.0 27.7 %all-reduce = (f32[16,128]{1,0:T(8,128)S(1)}, f32[]{:T(128)}) all-reduce(f32[16,128]{1,0:T(8,128)S(1)} %fusion.68, f32[]{:T(128)} %add_reduce_fusion.1), channel_id=1, replica_groups=mesh['gx'=16,'gy_0'=4,'gy_1'=4,'gy_2'=2] {'gx'}, use_global_device_ids=true, to_apply=%region_13.14 | all-reduce | flops 2049 | bytes 16392 | tf_op jit(solution)/shard_map/psum | solution.py:34
  435.7 10.2 %all-reduce.2 = (f32[16,128]{1,0:T(8,128)S(1)}, f32[]{:T(128)}) all-reduce(f32[16,128]{1,0:T(8,128)S(1)} %get-tuple-element.360, f32[]{:T(128)} %get-tuple-element.361), channel_id=1, replica_groups=mesh['gx'=16,'gy_0'=4,'gy_1'=4,'gy_2'=2] {'gy_0'}, use_global_device_ids=true, to_apply=%region_14.15 | all-reduce | flops 2049 | bytes 16392 | tf_op jit(solution)/shard_map/psum | solution.py:34
  445.9 9.4 %all-reduce.1 = (f32[16,128]{1,0:T(8,128)S(1)}, f32[]{:T(128)}) all-reduce(f32[16,128]{1,0:T(8,128)S(1)} %get-tuple-element.364, f32[]{:T(128)} %get-tuple-element.365), channel_id=1, replica_groups=mesh['gx'=16,'gy_0'=4,'gy_1'=4,'gy_2'=2] {'gy_1'}, use_global_device_ids=true, to_apply=%region_15.16 | all-reduce | flops 2049 | bytes 16392 | tf_op jit(solution)/shard_map/psum | solution.py:34
  455.3 18.9 %all-reduce.3 = (f32[16,128]{1,0:T(8,128)S(1)}, f32[]{:T(128)}) all-reduce(f32[16,128]{1,0:T(8,128)S(1)} %get-tuple-element.362, f32[]{:T(128)} %get-tuple-element.363), channel_id=1, replica_groups=mesh['gx'=16,'gy_0'=4,'gy_1'=4,'gy_2'=2] {'gy_2'}, use_global_device_ids=true, to_apply=%region_16.17 | all-reduce | flops 2049 | bytes 16392 | tf_op jit(solution)/shard_map/psum | solution.py:34
  474.8 2.5 fusion.54
  477.3 1.0 all-gather.4.cloned.1.call-done
  478.3 3.9 reduce.5
  (273 shorter events, 96.9 us)
Async XLA Ops:
  9.7 16.0 %copy-start.1 = (bf16[64,4096]{1,0:T(8,128)(2,1)S(1)}, bf16[64,4096]{1,0:T(8,128)(2,1)}, u32[]{:S(2)}) copy-start(bf16[64,4096]{1,0:T(8,128)(2,1)} %param.12) | copy-start | bytes 1572868
  9.7 107.8 %all-to-all-start = ((bf16[16,1,12,4096]{3,2,1,0:T(8,128)(2,1)}), bf16[16,1,12,4096]{3,2,1,0:T(8,128)(2,1)}, u32[]{:S(2)}, u32[]{:S(2)}) async-start(bf16[16,1,12,4096]{3,2,1,0:T(8,128)(2,1)} %stack.2), calls=%async_computation | async-start | bytes 4194304 | tf_op jit(solution)/shard_map/all_to_all | solution.py:98
  25.6 452.7 %all-gather.4.cloned.1.call-start = ((), (), s32[]{:S(2)}) async-start(), calls=%async_computation.2 | async-start | bytes 8650752 | tf_op jit(solution)/shard_map/all_gather | solution.py:30
  28.3 0.8 copy-start.2
  38.1 3.9 copy-start.5
  38.1 3.9 copy-start.6
  38.1 4.2 copy-start.3
  38.1 4.2 copy-start
  38.1 4.2 copy-start.4
Sparse Core Ops, SparseCore 0:
  407.3 70.9 all-gather.3
